TPU v7x, 32 devices: a whole 2x2x4 slice. The times are simulated.
32 devices in a mesh: tm: 8 (over y, x, core), row: 4 (over z).
Axes of the slice: x: 2, y: 2, z: 4, core: 2. Of those that a mesh axis runs over, the one named last changes fastest.
Arguments:
- latent: bfloat16 [16, 8, 40, 2240], P('tm', 'row'), may hold values from -6 to 6
- query_raw: bfloat16 [16, 8, 40, 2240], P('tm', 'row'), may hold values from -6 to 6
- key_raw: bfloat16 [16, 8, 40, 2240], P('tm', 'row'), may hold values from -12 to 12
- value_raw: bfloat16 [16, 8, 40, 2240], P('tm', 'row'), may hold values from -12 to 12
- query_gain: float32 [2240], replicated, may hold values from 0.4 to 2.5
- key_gain: float32 [2240], replicated, may hold values from 0.4 to 2.5
- space_kernel: float32 [3, 3, 2240], replicated, may hold values from -2 to 2
- time_kernel: float32 [3, 2240], replicated, may hold values from -3.5 to 3.5
- first_weight: bfloat16 [2240, 2048], P('tm', 'row'), may hold values from -0.125 to 0.125
- first_bias: float32 [2048], replicated, may hold values from -3 to 3
- second_weight: bfloat16 [2048, 1280], P('row', 'tm'), may hold values from -0.125 to 0.125
- second_bias: float32 [1280], replicated, may hold values from -3 to 3
- target_keys: bfloat16 [16, 256, 1280], P('tm', 'row'), may hold values from -410 to 410
- target_values: bfloat16 [16, 256, 1280], P('tm', 'row'), may hold values from -12 to 12
Outputs:
- blended: bfloat16 [16, 8, 40, 2240], P('tm', 'row')
- attended: bfloat16 [16, 8, 40, 1280], P('tm', 'row')
All inputs are finite; a program needn't handle non-finite values.
Results may differ from a plain program's by a relative error of at most 0.01545.
The roundings to bfloat16 on the way count: a program that leaves them out, or rounds other values in their place, can miss the bound.
Values may be sent and summed in bfloat16 or wider, within the bound.
A program may use at most 128 MiB of HBM per device.

v0:
```python
import jax
import jax.numpy as jnp
from jax import lax
from jax.sharding import PartitionSpec as P

HEADS = 70
HEAD_DIM = 32
AHEADS = 16
AHEAD_DIM = 80


def prefix(value, axis, combine, identity):
    length, index = (lax.axis_size(axis), lax.axis_index(axis))
    everything = jax.tree.map(lambda part: lax.all_gather(part, axis), value)
    start = jax.tree.map(
        lambda part, zero: jnp.broadcast_to(jnp.asarray(zero, part.dtype), part.shape),
        value,
        identity,
    )

    def lap(k, before):
        reached = k < index
        new = combine(before, jax.tree.map(lambda part: part[k], everything))
        return jax.tree.map(lambda a, b: jnp.where(reached, a, b), new, before)

    return lax.fori_loop(0, length, lap, start)


def extended(block, sides, width):
    for axis, dim in sides:
        count = lax.axis_size(axis)
        forward = [(i, i + 1) for i in range(count - 1)]
        backward = [(target, source) for source, target in forward]
        low = lax.ppermute(
            lax.slice_in_dim(block, block.shape[dim] - width, None, axis=dim), axis, forward
        )
        high = lax.ppermute(lax.slice_in_dim(block, 0, width, axis=dim), axis, backward)
        block = jnp.concatenate([low, block, high], axis=dim)
    return block


def head_features(source, scaling):
    values = source.astype(jnp.float32).reshape(source.shape[:-1] + (HEADS, HEAD_DIM))
    mean_square = jnp.maximum(jnp.mean(values * values, axis=-1, keepdims=True), 0.25)
    return jax.nn.relu(values * lax.rsqrt(mean_square) * scaling.reshape(HEADS, HEAD_DIM))


def add_pair(earlier, later):
    return (earlier[0] + later[0], earlier[1] + later[1])


def contraction(left, piece):
    return jnp.dot(left, piece, preferred_element_type=jnp.float32)


def frame_softmax(query_split, key_split, value_split):
    score_scale = 1.0 / AHEAD_DIM**0.5
    scores = (
        jnp.einsum("cqgd,ckgd->cgqk", query_split, key_split, preferred_element_type=jnp.float32)
        * score_scale
    )
    row_max = jnp.max(scores, axis=-1, keepdims=True)
    weights = jnp.exp(scores - row_max)
    row_total = jnp.sum(weights, axis=-1)
    result = jnp.einsum(
        "cgqk,ckgd->cqgd",
        weights.astype(jnp.bfloat16),
        value_split,
        preferred_element_type=jnp.float32,
    )
    return result / jnp.transpose(row_total, (0, 2, 1))[..., None]


def per_device(
    latent,
    query_raw,
    key_raw,
    value_raw,
    query_gain,
    key_gain,
    space_kernel,
    time_kernel,
    first_weight,
    first_bias,
    second_weight,
    second_bias,
    target_keys,
    target_values,
):
    frames_here, rows_here, cols_here, model_width = latent.shape
    token_count = frames_here * rows_here * cols_here
    query_feat = head_features(query_raw, query_gain)
    key_feat = head_features(key_raw, key_gain)
    value_feat = value_raw.astype(jnp.float32).reshape(key_feat.shape)
    local_state = jnp.einsum(
        "crwhd,crwhe->dhe", key_feat, value_feat, precision=lax.Precision.HIGHEST
    ).reshape(HEAD_DIM, model_width)
    local_keys = jnp.sum(key_feat, axis=(0, 1, 2)).reshape(model_width)
    block_state, block_keys = lax.psum((local_state, local_keys), "row")
    earlier_state, earlier_keys = prefix(
        (block_state, block_keys),
        "tm",
        add_pair,
        (jnp.zeros_like(block_state), jnp.zeros_like(block_keys)),
    )
    key_state = (earlier_state + block_state).reshape(HEAD_DIM, HEADS, HEAD_DIM)
    key_total = (earlier_keys + block_keys).reshape(HEADS, HEAD_DIM)
    numerator = jnp.einsum(
        "crwhd,dhe->crwhe", query_feat, key_state, precision=lax.Precision.HIGHEST
    )
    denominator = (
        jnp.einsum("crwhd,hd->crwh", query_feat, key_total, precision=lax.Precision.HIGHEST) + 1e-06
    )
    linear_out = (numerator / denominator[..., None]).reshape(latent.shape)
    hidden_in = (latent.astype(jnp.float32) + linear_out).astype(jnp.bfloat16)
    time_padded = extended(hidden_in, (("tm", 0),), 1)
    row_padded = extended(hidden_in, (("row", 1),), 1)
    row_padded = jnp.pad(row_padded, ((0, 0), (0, 0), (1, 1), (0, 0)))
    center = hidden_in.astype(jnp.float32)
    spatial = jnp.zeros(center.shape, jnp.float32)
    for shift_row in range(3):
        for shift_col in range(3):
            spatial = spatial + space_kernel[shift_row, shift_col] * row_padded[
                :, shift_row : shift_row + rows_here, shift_col : shift_col + cols_here
            ].astype(jnp.float32)
    temporal = jnp.zeros(center.shape, jnp.float32)
    for shift_time in range(3):
        temporal = temporal + time_kernel[shift_time] * time_padded[
            shift_time : shift_time + frames_here
        ].astype(jnp.float32)
    blended = (center + spatial + temporal).astype(jnp.bfloat16)
    tokens = blended.reshape(token_count, model_width)
    first_full = lax.all_gather(first_weight, "row", axis=1, tiled=True)
    linear_part = contraction(tokens, lax.all_gather(first_full, "tm", axis=0, tiled=True))
    hidden_units = jax.nn.silu(linear_part + first_bias).astype(jnp.bfloat16)
    second_full = lax.all_gather(second_weight, "row", axis=0, tiled=True)
    queries = (
        jnp.dot(
            hidden_units,
            lax.all_gather(second_full, "tm", axis=1, tiled=True),
            preferred_element_type=jnp.float32,
        )
        + second_bias
    ).astype(jnp.bfloat16)
    frame_tokens = rows_here * cols_here
    feature_count = queries.shape[1]
    query_grid = queries.reshape(frames_here, frame_tokens, feature_count)
    query_moved = lax.all_to_all(query_grid, "row", split_axis=2, concat_axis=1, tiled=True)
    key_moved, value_moved = (
        lax.all_to_all(target_keys, "row", split_axis=2, concat_axis=1, tiled=True),
        lax.all_to_all(target_values, "row", split_axis=2, concat_axis=1, tiled=True),
    )
    heads_here = AHEADS // lax.axis_size("row")
    result = frame_softmax(
        query_moved.reshape(frames_here, query_moved.shape[1], heads_here, AHEAD_DIM),
        key_moved.reshape(frames_here, key_moved.shape[1], heads_here, AHEAD_DIM),
        value_moved.reshape(frames_here, value_moved.shape[1], heads_here, AHEAD_DIM),
    )
    result = result.reshape(frames_here, query_moved.shape[1], query_moved.shape[2]).astype(
        jnp.bfloat16
    )
    attended = lax.all_to_all(result, "row", split_axis=1, concat_axis=2, tiled=True)
    attended = attended.reshape(frames_here, rows_here, cols_here, feature_count)
    return (blended, attended)


def solution(mesh):
    return jax.shard_map(
        per_device,
        mesh=mesh,
        in_specs=(
            P("tm", "row", None, None),
            P("tm", "row", None, None),
            P("tm", "row", None, None),
            P("tm", "row", None, None),
            P(),
            P(),
            P(),
            P(),
            P("tm", "row"),
            P(),
            P("row", "tm"),
            P(),
            P("tm", "row", None),
            P("tm", "row", None),
        ),
        out_specs=(P("tm", "row", None, None), P("tm", "row", None, None)),
        check_vma=False,
    )
```

profile of v0, /device:TPU:0, one launch (start us, length us, event | category | flops | bytes accessed | tf_op | source)
XLA Modules:
  0.0 353.0 jit_solution(5455489802273195994)
XLA Ops:
  7.2 4.9 %reshape.93 = f32[2,2,40,70,32]{4,3,2,1,0:T(8,128)} reshape(bf16[2,2,40,2240]{3,2,1,0:T(8,128)(2,1)} %param.18) | data formatting | bytes 2150400 | tf_op jit(solution)/shard_map/reshape | solution.py:43
  12.2 5.5 %multiply_reduce_fusion.1 = f32[2,2,40,70]{3,2,1,0:T(8,128)S(1)} fusion(f32[2,2,40,70,32]{4,3,2,1,0:T(8,128)} %reshape.93), kind=kLoop, calls=%fused_computation.6 | loop fusion | flops 705600 | bytes 1478400 | tf_op jit(solution)/shard_map/reduce_sum | solution.py:44
  21.4 4.2 %multiply_maximum_fusion.1 = f32[2,2,40,70,32]{4,3,2,1,0:T(8,128)S(1)} fusion(f32[2,2,40,70,32]{4,3,2,1,0:T(8,128)} %reshape.93, f32[70,32]{1,0:T(8,128)S(1)} %mul.185, f32[2,2,40,70]{3,2,1,0:T(8,128)S(1)} %maximum_rsqrt_fusion.1), kind=kLoop, calls=%fused_computation.5 | loop fusion | flops 1075200 | bytes 2920960 | tf_op jit(solution)/shard_map/jit(relu)/max | solution.py:45
  25.7 4.8 %fusion.21 = f32[32,70,32]{2,0,1:T(8,128)S(1)} fusion(bf16[2,2,40,70,32]{4,3,2,1,0:T(8,128)(2,1)S(1)} %reshape.94, f32[2,2,40,70,32]{4,3,2,1,0:T(8,128)S(1)} %multiply_maximum_fusion.1), kind=kOutput, calls=%fused_computation.40 | convolution fusion | flops 137625600 | bytes 2437120 | tf_op jit(solution)/shard_map/crwhd,crwhe->dhe/dot_general | solution.py:95
  36.7 4.1 %mul.188 = f32[2,2,40,2240]{3,2,1,0:T(8,128)S(1)} reshape(f32[2,2,40,70,32]{4,3,2,1,0:T(8,128)} %mul.183) | data formatting | bytes 2867200 | tf_op jit(solution)/shard_map/mul | solution.py:45
  42.4 20.5 %psum.15 = f32[2240]{0:T(1024)S(1)} all-reduce(f32[2240]{0:T(1024)S(1)} %maximum_reduce_fusion), channel_id=1, replica_groups=mesh['tm'=8,'row'=4] {'row'}, use_global_device_ids=true, to_apply=%region_3.4 | all-reduce | flops 2240 | bytes 17920 | tf_op jit(solution)/shard_map/psum | solution.py:99
  64.0 6.9 %all-reduce.5.cloned.1.call-done = f32[32,2240]{1,0:T(8,128)} async-done(((f32[32,2240]{1,0:T(8,128)}), f32[32,2240]{1,0:T(8,128)}) %all-reduce.5.cloned.1.call-update) | async-done | bytes 286736 | tf_op jit(solution)/shard_map/psum | solution.py:99
  71.0 20.2 %all_gather.30 = bf16[2048,160]{0,1:T(8,128)(2,1)} all-gather(bf16[512,160]{0,1:T(8,128)(2,1)S(1)} %copy-done.10), channel_id=1, replica_groups=mesh['tm'=8,'row'=4] {'row'}, dimensions={0}, use_global_device_ids=true | all-gather | bytes 819200 | tf_op jit(solution)/shard_map/all_gather | solution.py:136
  91.3 13.1 %all-gather.7.cloned.1.call-done = bf16[280,2048]{1,0:T(8,128)(2,1)} async-done(((bf16[280,512]{1,0:T(8,128)(2,1)}), bf16[280,2048]{1,0:T(8,128)(2,1)}) %all-gather.7.cloned.1.call-update) | async-done | bytes 1146896 | tf_op jit(solution)/shard_map/all_gather | solution.py:133
  113.8 5.6 %multiply_reduce_fusion = f32[2,2,40,70]{3,2,1,0:T(8,128)S(1)} fusion(f32[2,2,40,70,32]{4,3,2,1,0:T(8,128)} %reshape.108), kind=kLoop, calls=%fused_computation.4 | loop fusion | flops 705600 | bytes 1478400 | tf_op jit(solution)/shard_map/reduce_sum | solution.py:44
  123.2 6.0 %copy.55 = f32[2,2,40,70,32]{2,4,1,0,3:T(8,128)} copy(f32[2,2,40,70,32]{4,3,2,1,0:T(8,128)} %multiply_maximum_fusion) | data formatting | bytes 2867200 | tf_op jit(solution)/shard_map/jit(relu)/max | solution.py:45
  131.3 26.3 %all-reduce.7.cloned.1.call-done = f32[17920]{0:T(1024)} async-done(((f32[17920]{0:T(1024)}), f32[17920]{0:T(1024)}) %all-reduce.7.cloned.1.call-update) | async-done | bytes 71696
  158.5 31.2 %all-gather.13.cloned.1.call-done = f32[256,2240]{1,0:T(8,128)} async-done(((f32[32,2240]{1,0:T(8,128)}), f32[256,2240]{1,0:T(8,128)}) %all-gather.13.cloned.1.call-update) | async-done | bytes 2293776 | tf_op jit(solution)/shard_map/all_gather | solution.py:14
  189.7 9.1 %while.16 = (s32[]{:T(128)}, f32[32,2240]{1,0:T(8,128)S(1)}, f32[2240]{0:T(1024)S(1)}, s32[]{:T(128)}, f32[8,32,2240]{2,1,0:T(8,128)}, /*index=5*/f32[8,2240]{1,0:T(8,128)S(1)}, s32[]{:T(128)}, s32[]{:T(128)}) while((s32[]{:T(128)}, f32[32,2240]{1,0:T(8,128)S(1)}, f32[2240]{0:T(1024)S(1)}, s32[]{:T(128)}, ...), condition=%wide.region_5.6_spmd.clone, body=%wide.region_4.5_spmd.clone.sunk | while | flops 221764 | bytes 905075 | solution.py:26
  199.4 5.0 %fusion.40 = f32[70,1,2,2,40]{4,1,3,2,0:T(1,128)S(1)} fusion(f32[70,32,1,1,1]{1,2,4,3,0:T(1,128)S(1)} %reshape.121, f32[2,2,40,70,32]{2,4,1,0,3:T(8,128)} %copy.55), kind=kOutput, calls=%fused_computation.74 | convolution fusion | flops 4300800 | bytes 1487360 | tf_op jit(solution)/shard_map/crwhd,hd->crwh/dot_general | solution.py:112
  204.4 5.4 %bitcast_divide_fusion = f32[2,2,40,70,32]{2,4,1,0,3:T(8,128)} fusion(f32[2,2,40,70]{2,1,0,3:T(2,128)S(1)} %add_bitcast_fusion, f32[32,70,32,1,1]{0,2,4,3,1:T(8,128)S(1)} %bitcast.78, f32[2,2,40,70,32]{2,4,1,0,3:T(8,128)S(1)} %copy-done.1), kind=kOutput, calls=%fused_computation.11 | convolution fusion | flops 137984000 | bytes 3198720 | tf_op jit(solution)/shard_map/crwhd,dhe->crwhe/dot_general | solution.py:108
  209.8 6.1 %copy.56 = f32[2,2,40,70,32]{4,3,2,1,0:T(8,128)} copy(f32[2,2,40,70,32]{2,4,1,0,3:T(8,128)} %bitcast_divide_fusion) | data formatting | bytes 2867200 | tf_op jit(solution)/shard_map/div | solution.py:114
  215.9 4.1 %reshape.100 = f32[2,2,40,2240]{3,2,1,0:T(8,128)S(1)} reshape(f32[2,2,40,70,32]{4,3,2,1,0:T(8,128)} %copy.56) | data formatting | bytes 2867200 | tf_op jit(solution)/shard_map/reshape | solution.py:114
  232.1 4.1 %collective-permute-done.1 = bf16[2,1,40,2240]{3,2,1,0:T(8,128)(2,1)S(1)} collective-permute-done((bf16[2,1,40,2240]{3,2,1,0:T(8,128)(2,1)S(1)}, bf16[2,1,40,2240]{3,2,1,0:T(8,128)(2,1)S(1)}, u32[]{:S(2)}, u32[]{:S(2)}) %collective-permute-start.1) | collective-permute-done | bytes 358432 | tf_op jit(solution)/shard_map/ppermute | solution.py:37
  242.6 49.8 %all-gather.9.cloned.1.call-done = bf16[2240,2048]{1,0:T(8,128)(2,1)} async-done(((bf16[280,2048]{1,0:T(8,128)(2,1)}), bf16[2240,2048]{1,0:T(8,128)(2,1)}) %all-gather.9.cloned.1.call-update) | async-done | bytes 9175056 | tf_op jit(solution)/shard_map/all_gather | solution.py:134
  292.4 8.6 %fusion.4 = bf16[160,1280]{1,0:T(8,128)(2,1)S(1)} fusion(bf16[2048,1280]{0,1:T(8,128)(2,1)} %all-gather.11.cloned.1.call-done, bf16[160,2240]{1,0:T(8,128)(2,1)S(1)} %bitcast.80, bf16[2240,2048]{1,0:T(8,128)(2,1)} %all-gather.9.cloned.1.call-done, f32[2048]{0:T(1024)S(1)} %copy-done.15, f32[1280]{0:T(1024)S(1)} %copy-done.16), kind=kOutput, calls=%fused_computation.18 | convolution fusion | flops 2309242880 | bytes 15557632 | tf_op jit(solution)/shard_map/dot_general | solution.py:138
  302.2 4.6 %all-to-all-start = ((bf16[2,80,1280]{1,0,2:T(2,128)(2,1)}), bf16[2,80,1280]{1,0,2:T(2,128)(2,1)S(1)}, u32[]{:S(2)}, u32[]{:S(2)}) async-start(bf16[2,80,1280]{1,0,2:T(2,128)(2,1)} %copy.57), calls=%async_computation | async-start | bytes 1310720 | tf_op jit(solution)/shard_map/all_to_all | solution.py:148
  309.3 15.2 %all-to-all-done = bf16[2,80,1280]{1,0,2:T(2,128)(2,1)S(1)} async-done(((bf16[2,80,1280]{1,0,2:T(2,128)(2,1)}), bf16[2,80,1280]{1,0,2:T(2,128)(2,1)S(1)}, u32[]{:S(2)}, u32[]{:S(2)}) %all-to-all-start) | async-done | bytes 409632 | tf_op jit(solution)/shard_map/all_to_all | solution.py:148
  329.0 15.8 %all_to_all.60 = bf16[2,320,320]{2,0,1:T(2,128)(2,1)S(1)} all-to-all(bf16[2,320,320]{2,0,1:T(2,128)(2,1)S(1)} %copy.67), channel_id=1, replica_groups=mesh['tm'=8,'row'=4] {'row'}, dimensions={1} | all-to-all | bytes 819200 | tf_op jit(solution)/shard_map/all_to_all | solution.py:162
  (133 shorter events, 65.3 us)
Async XLA Ops:
  7.2 63.8 %all-reduce.5.cloned.1.call-start = ((), (), s32[]{:S(2)}) async-start(), calls=%async_computation.4 | async-start | bytes 589824 | tf_op jit(solution)/shard_map/psum | solution.py:99
  12.1 5.5 %copy-start.12 = (f32[2240]{0:T(1024)S(1)}, f32[2240]{0:T(1024)}, u32[]{:S(2)}) copy-start(f32[2240]{0:T(1024)} %param.21) | copy-start | bytes 26884
  32.2 72.2 %all-gather.7.cloned.1.call-start = ((), (), s32[]{:S(2)}) async-start(), calls=%async_computation.5 | async-start | bytes 1433600 | tf_op jit(solution)/shard_map/all_gather | solution.py:133
  33.0 124.6 %all-reduce.7.cloned.1.call-start = ((), (), s32[]{:S(2)}) async-start(), calls=%async_computation.9 | async-start | bytes 147456
  36.7 5.4 %copy-start.2 = (bf16[2,2,40,2240]{3,2,1,0:T(8,128)(2,1)S(1)}, bf16[2,2,40,2240]{3,2,1,0:T(8,128)(2,1)}, u32[]{:S(2)}) copy-start(bf16[2,2,40,2240]{3,2,1,0:T(8,128)(2,1)} %param.18) | copy-start | bytes 2150404
  40.9 30.2 %copy-start.10 = (bf16[512,160]{0,1:T(8,128)(2,1)S(1)}, bf16[512,160]{0,1:T(8,128)(2,1)}, u32[]{:S(2)}) copy-start(bf16[512,160]{0,1:T(8,128)(2,1)} %param.26) | copy-start | bytes 491524
  42.4 62.0 %copy-start.7 = (bf16[2,64,1280]{2,1,0:T(8,128)(2,1)S(1)}, bf16[2,64,1280]{2,1,0:T(8,128)(2,1)}, u32[]{:S(2)}) copy-start(bf16[2,64,1280]{2,1,0:T(8,128)(2,1)} %param.28) | copy-start | bytes 983044
  64.0 125.7 %all-gather.13.cloned.1.call-start = ((), (), s32[]{:S(2)}) async-start(), calls=%async_computation.8 | async-start | bytes 2654208 | tf_op jit(solution)/shard_map/all_gather | solution.py:14
  71.0 171.7 %all-gather.11.cloned.1.call-start = ((), (), s32[]{:S(2)}) async-start(), calls=%async_computation.7 | async-start | bytes 5898240 | tf_op jit(solution)/shard_map/all_gather | solution.py:140
  91.3 201.1 %all-gather.9.cloned.1.call-start = ((), (), s32[]{:S(2)}) async-start(), calls=%async_computation.6 | async-start | bytes 10321920 | tf_op jit(solution)/shard_map/all_gather | solution.py:134
  104.4 5.4 %copy-start.4 = (bf16[2,2,40,2240]{3,2,1,0:T(8,128)(2,1)S(1)}, bf16[2,2,40,2240]{3,2,1,0:T(8,128)(2,1)}, u32[]{:S(2)}) copy-start(bf16[2,2,40,2240]{3,2,1,0:T(8,128)(2,1)} %param.17) | copy-start | bytes 2150404
  106.2 132.8 %all-to-all-start.1 = ((bf16[4,2,20480]{2,1,0:T(2,128)(2,1)}), bf16[4,2,20480]{2,1,0:T(2,128)(2,1)S(1)}, u32[]{:S(2)}, u32[]{:S(2)}) async-start(bf16[4,2,20480]{2,1,0:T(2,128)(2,1)} %reshape.136), calls=%async_computation.1 | async-start | bytes 655360 | tf_op jit(solution)/shard_map/all_to_all | solution.py:150
  113.8 5.6 %copy-start = (f32[2,2,40,70,32]{4,3,2,1,0:T(8,128)S(1)}, f32[2,2,40,70,32]{4,3,2,1,0:T(8,128)}, u32[]{:S(2)}) copy-start(f32[2,2,40,70,32]{4,3,2,1,0:T(8,128)} %reshape.108) | copy-start | bytes 4300804
  123.2 6.1 %copy-start.8 = (bf16[2,64,1280]{2,1,0:T(8,128)(2,1)S(1)}, bf16[2,64,1280]{2,1,0:T(8,128)(2,1)}, u32[]{:S(2)}) copy-start(bf16[2,64,1280]{2,1,0:T(8,128)(2,1)} %param.29) | copy-start | bytes 983044
  189.7 9.3 %copy-start.3 = (f32[32,2240]{1,0:T(8,128)S(1)}, f32[32,2240]{1,0:T(8,128)}, u32[]{:S(2)}) copy-start(f32[32,2240]{1,0:T(8,128)} %all-reduce.5.cloned.1.call-done) | copy-start | bytes 860164
  220.3 11.8 %collective-permute-start = (bf16[2,1,40,2240]{3,2,1,0:T(8,128)(2,1)S(1)}, bf16[2,1,40,2240]{3,2,1,0:T(8,128)(2,1)S(1)}, u32[]{:S(2)}, u32[]{:S(2)}) collective-permute-start(bf16[2,1,40,2240]{3,2,1,0:T(8,128)(2,1)S(1)} %get-tuple-element.159), channel_id=1, source_target_pairs={{0,1},{1,2},{2,3},{4,5},{5,6},{6,7},{8,9},{9,10},{10,11},{12,13},{... | collective-permute-start | bytes 1075208 | tf_op jit(solution)/shard_map/ppermute | solution.py:34
  223.8 12.4 %collective-permute-start.1 = (bf16[2,1,40,2240]{3,2,1,0:T(8,128)(2,1)S(1)}, bf16[2,1,40,2240]{3,2,1,0:T(8,128)(2,1)S(1)}, u32[]{:S(2)}, u32[]{:S(2)}) collective-permute-start(bf16[2,1,40,2240]{3,2,1,0:T(8,128)(2,1)S(1)} %get-tuple-element.160), channel_id=1, source_target_pairs={{1,0},{2,1},{3,2},{5,4},{6,5},{7,6},{9,8},{10,9},{11,10},{13,12},{... | collective-permute-start | bytes 1075208 | tf_op jit(solution)/shard_map/ppermute | solution.py:37
  225.1 11.6 %collective-permute-start.2 = (bf16[1,2,40,2240]{3,2,1,0:T(8,128)(2,1)S(1)}, bf16[1,2,40,2240]{3,2,1,0:T(8,128)(2,1)S(1)}, u32[]{:S(2)}, u32[]{:S(2)}) collective-permute-start(bf16[1,2,40,2240]{3,2,1,0:T(8,128)(2,1)S(1)} %get-tuple-element.161), channel_id=1, source_target_pairs={{0,4},{4,8},{8,12},{12,16},{16,20},{20,24},{24,28},{1,5},{5,9},{9,... | collective-permute-start | bytes 1075208 | tf_op jit(solution)/shard_map/ppermute | solution.py:34
  227.1 9.6 %collective-permute-start.3 = (bf16[1,2,40,2240]{3,2,1,0:T(8,128)(2,1)S(1)}, bf16[1,2,40,2240]{3,2,1,0:T(8,128)(2,1)S(1)}, u32[]{:S(2)}, u32[]{:S(2)}) collective-permute-start(bf16[1,2,40,2240]{3,2,1,0:T(8,128)(2,1)S(1)} %get-tuple-element.162), channel_id=1, source_target_pairs={{4,0},{8,4},{12,8},{16,12},{20,16},{24,20},{28,24},{5,1},{9,5},{13... | collective-permute-start | bytes 1075208 | tf_op jit(solution)/shard_map/ppermute | solution.py:37
  236.7 55.6 %copy-start.15 = (f32[2048]{0:T(1024)S(1)}, f32[2048]{0:T(1024)}, u32[]{:S(2)}) copy-start(f32[2048]{0:T(1024)} %param.25) | copy-start | bytes 24580
  236.7 55.6 %copy-start.16 = (f32[1280]{0:T(1024)S(1)}, f32[1280]{0:T(1024)}, u32[]{:S(2)}) copy-start(f32[1280]{0:T(1024)} %param.27) | copy-start | bytes 15364
  238.9 62.1 %copy-start.5 = (bf16[2,2,40,2240]{3,2,1,0:T(8,128)(2,1)}, bf16[2,2,40,2240]{3,2,1,0:T(8,128)(2,1)S(1)}, u32[]{:S(2)}) copy-start(bf16[2,2,40,2240]{3,2,1,0:T(8,128)(2,1)S(1)} %fusion.18) | copy-start | bytes 2150404
  239.0 63.3 %all-to-all-start.2 = ((bf16[4,2,20480]{2,1,0:T(2,128)(2,1)}), bf16[4,2,20480]{2,1,0:T(2,128)(2,1)S(1)}, u32[]{:S(2)}, u32[]{:S(2)}) async-start(bf16[4,2,20480]{2,1,0:T(2,128)(2,1)} %reshape.138), calls=%async_computation.2 | async-start | bytes 655360 | tf_op jit(solution)/shard_map/all_to_all | solution.py:151
  302.2 22.3 %all-to-all-start = ((bf16[2,80,1280]{1,0,2:T(2,128)(2,1)}), bf16[2,80,1280]{1,0,2:T(2,128)(2,1)S(1)}, u32[]{:S(2)}, u32[]{:S(2)}) async-start(bf16[2,80,1280]{1,0,2:T(2,128)(2,1)} %copy.57), calls=%async_computation | async-start | bytes 1310720 | tf_op jit(solution)/shard_map/all_to_all | solution.py:148
  (7 other events, 21.5 us)
Sparse Core Ops, SparseCore 0:
  32.3 38.5 all-reduce.4
  72.5 31.8 all-gather.6
  108.1 49.4 all-reduce.6
  159.4 30.2 all-gather.12
  191.6 41.1 all-gather.10
  234.6 57.7 all-gather.8
where the time goes:
time: 354 us; the launch traced here: 353 us
  waiting for transfers between devices  151 us (43%)
  blocking collectives  56.5 us (16%)
  local copies, waits for them, and re-layouts  52.6 us (15%)
  other arithmetic  31.7 us (9%)
  matrix products  25.4 us (7%)
  starting transfers between devices  20.4 us (6%)
  between operations  15.3 us (4%)
    all_gather x1, waiting for transfers between devices, per_device(): lax.all_gather(first_full, 'tm', axis=0, tiled=True)  49.8 us
    all_gather x1, waiting for transfers between devices, prefix(): everything = jax.tree.map(lambda part: lax.all_gather(part, axis), value)  31.2 us
    unnamed x7, waiting for transfers between devices  27 us
    psum x1, blocking collectives, per_device(): block_state, block_keys = lax.psum((local_state, local_keys), 'row')  20.5 us
    all_gather x1, blocking collectives, per_device(): second_full = lax.all_gather(second_weight, 'row', axis=0, tiled=True)  20.2 us
    all_to_all x1, blocking collectives, per_device(): lax.all_to_all(result, 'row', split_axis=1, concat_axis=2, tiled=True)  15.8 us
    all_to_all x1, waiting for transfers between devices, per_device(): lax.all_to_all(query_grid, 'row', split_axis=2, concat_axis=1, tiled=True)  15.2 us
    all_gather x1, waiting for transfers between devices, per_device(): first_full = lax.all_gather(first_weight, 'row', axis=1, tiled=True)  13.1 us
  transfers between devices with their start and end apart: 13, of which 8 were waited for; matrix products, arithmetic and copies ran while one was open for 22% of the time, Pallas kernels for 0%

commit v1 on v0

v1 whole, which is shorter than its diff:
```python
import functools

import jax
import jax.numpy as jnp
from jax import lax
from jax.experimental import pallas as pl
from jax.experimental.pallas import tpu as pltpu
from jax.sharding import PartitionSpec as P

HEADS = 70
HEAD_DIM = 32
AHEADS = 16
AHEAD_DIM = 80
LANES = 128
SLAB = 48
STATE_TYPE = jnp.float32
F32, BF16 = jnp.float32, jnp.bfloat16
MESH = pl.DeviceIdType.MESH


def groups_of(width):
    return [(start, min(LANES, width - start)) for start in range(0, width, LANES)]


def same_head(size):
    row = lax.broadcasted_iota(jnp.int32, (size, size), 0) // HEAD_DIM
    col = lax.broadcasted_iota(jnp.int32, (size, size), 1) // HEAD_DIM
    return (row == col).astype(F32)


def parts(value):
    high = value.astype(BF16)
    return high, (value - high.astype(F32)).astype(BF16)


def dot(left, right):
    return jnp.dot(left, right, preferred_element_type=F32)


def token_dot(left, right):
    return lax.dot_general(left, right, (((0,), (0,)), ((), ())), preferred_element_type=F32)


def head_sums(value, ones):
    high, low = parts(value)
    return dot(high, ones) + dot(low, ones)


def features(source, gain, ones):
    values = source.astype(F32)
    mean_square = jnp.maximum(head_sums(values * values, ones) * (1.0 / HEAD_DIM), 0.25)
    return jnp.maximum(values * lax.rsqrt(mean_square) * gain, 0.0)


def front_kernel(
    count_t, count_r, frames, rows, cols,
    key_ref, value_ref, query_ref, latent_ref, key_gain, query_gain, space_ref, time_ref,
    out_ref,
    state, row_in, mine, before, final, hidden,
    rs_send, rs_recv, p_send, p_recv, g_send, g_recv, h_send, h_recv,
):
    me_t, me_r = lax.axis_index("tm"), lax.axis_index("row")
    width = key_ref.shape[1]
    groups = groups_of(width)
    per_part = -(-len(groups) // count_r)

    barrier = pltpu.get_barrier_semaphore()

    def greet_t(k, carry):
        pl.semaphore_signal(
            barrier, inc=1, device_id={"tm": lax.rem(me_t + k, count_t)}, device_id_type=MESH
        )
        return carry

    lax.fori_loop(1, count_t, greet_t, 0)
    for k in range(1, count_r):
        pl.semaphore_signal(
            barrier, inc=1, device_id={"row": lax.rem(me_r + k, count_r)}, device_id_type=MESH
        )

    state[...] = jnp.zeros_like(state)
    for index, (start, size) in enumerate(groups):
        mask = same_head(size)
        ones = mask.astype(BF16)
        lanes = pl.ds(start, size)
        feat = features(key_ref[:, lanes], key_gain[:, lanes], ones)
        high, low = parts(feat)
        values = value_ref[:, lanes]
        outer = (token_dot(high, values) + token_dot(low, values)) * mask
        packed = outer[0:HEAD_DIM]
        for head in range(1, size // HEAD_DIM):
            packed = packed + outer[head * HEAD_DIM : (head + 1) * HEAD_DIM]
        sums = jnp.broadcast_to(jnp.sum(feat, axis=0, keepdims=True), (SLAB - HEAD_DIM, size))
        tail = lax.broadcasted_iota(jnp.int32, sums.shape, 0) == 0
        block = jnp.concatenate([packed, jnp.where(tail, sums, 0.0)], axis=0)
        state[index // per_part, :, pl.ds((index % per_part) * LANES, size)] = block.astype(
            STATE_TYPE
        )

    pl.semaphore_wait(barrier, count_t - 1 + count_r - 1)

    def row_copy(peer, slot):
        return pltpu.make_async_remote_copy(
            src_ref=state.at[peer], dst_ref=row_in.at[slot],
            send_sem=rs_send.at[peer], recv_sem=rs_recv.at[slot],
            device_id={"row": peer}, device_id_type=MESH,
        )

    for k in range(1, count_r):
        row_copy(lax.rem(me_r + k, count_r), me_r).start()
    total = state[me_r].astype(F32)
    for k in range(1, count_r):
        peer = lax.rem(me_r + k, count_r)
        row_copy(peer, peer).wait_recv()
        total = total + row_in[peer].astype(F32)
    mine[...] = total.astype(STATE_TYPE)

    def prefix_copy(peer, slot):
        return pltpu.make_async_remote_copy(
            src_ref=mine, dst_ref=before.at[slot],
            send_sem=p_send.at[peer], recv_sem=p_recv.at[slot],
            device_id={"tm": peer}, device_id_type=MESH,
        )

    def send_later(peer, carry):
        prefix_copy(peer, me_t).start()
        return carry

    lax.fori_loop(me_t + 1, count_t, send_later, 0)
    final[me_r] = total.astype(STATE_TYPE)

    def add_earlier(peer, carry):
        prefix_copy(peer, peer).wait_recv()
        final[me_r] = (final[me_r].astype(F32) + before[peer].astype(F32)).astype(STATE_TYPE)
        return carry

    lax.fori_loop(0, me_t, add_earlier, 0)

    def final_copy(peer, slot):
        return pltpu.make_async_remote_copy(
            src_ref=final.at[me_r], dst_ref=final.at[slot],
            send_sem=g_send.at[peer], recv_sem=g_recv.at[slot],
            device_id={"row": peer}, device_id_type=MESH,
        )

    def final_arrival(peer):
        return pltpu.make_async_remote_copy(
            src_ref=final.at[peer], dst_ref=final.at[peer],
            send_sem=g_send.at[peer], recv_sem=g_recv.at[peer],
            device_id={"row": peer}, device_id_type=MESH,
        )

    for k in range(1, count_r):
        final_copy(lax.rem(me_r + k, count_r), me_r).start()
    for k in range(1, count_r):
        final_arrival(lax.rem(me_r + k, count_r)).wait_recv()

    for index, (start, size) in enumerate(groups):
        mask = same_head(size)
        ones = mask.astype(BF16)
        lanes = pl.ds(start, size)
        held = final[index // per_part, :, pl.ds((index % per_part) * LANES, size)].astype(F32)
        feat = features(query_ref[:, lanes], query_gain[:, lanes], ones)
        high, low = parts(feat)
        table = jnp.concatenate([held[0:HEAD_DIM]] * (size // HEAD_DIM), axis=0) * mask
        table_high, table_low = parts(table)
        numerator = dot(high, table_high) + dot(low, table_high) + dot(high, table_low)
        denominator = head_sums(feat * held[HEAD_DIM : HEAD_DIM + 1], ones) + 1e-06
        mixed = latent_ref[:, lanes].astype(F32) + numerator / denominator
        for f in range(frames):
            for r in range(rows):
                at = (f * rows + r) * cols
                padded = jnp.concatenate(
                    [mixed[at : at + cols], jnp.zeros((SLAB - cols, size), F32)], axis=0
                )
                hidden[f + 1, r + 1, :, lanes] = padded.astype(BF16)

    body_f, body_r = pl.ds(1, frames), pl.ds(1, rows)
    moves = (
        ("tm", me_t, count_t, -1, hidden.at[1, body_r], hidden.at[frames + 1, body_r]),
        ("tm", me_t, count_t, 1, hidden.at[frames, body_r], hidden.at[0, body_r]),
        ("row", me_r, count_r, -1, hidden.at[body_f, 1], hidden.at[body_f, rows + 1]),
        ("row", me_r, count_r, 1, hidden.at[body_f, rows], hidden.at[body_f, 0]),
    )

    def halo(i):
        axis, me, count, step, source, target = moves[i]
        return pltpu.make_async_remote_copy(
            src_ref=source, dst_ref=target, send_sem=h_send.at[i], recv_sem=h_recv.at[i],
            device_id={axis: lax.rem(me + step + count, count)}, device_id_type=MESH,
        )

    def sends(i):
        _, me, count, step, _, _ = moves[i]
        return (me > 0) if step < 0 else (me < count - 1)

    def receives(i):
        _, me, count, step, _, _ = moves[i]
        return (me < count - 1) if step < 0 else (me > 0)

    for i in range(4):
        pl.when(sends(i))(halo(i).start)
    for i in range(4):
        target = moves[i][5]

        @pl.when(jnp.logical_not(receives(i)))
        def _():
            target[...] = jnp.zeros(target.shape, BF16)

    for i in range(4):
        pl.when(receives(i))(halo(i).wait_recv)

    for start, size in groups:
        lanes = pl.ds(start, size)
        taps = [space_ref[i : i + 1, lanes] for i in range(9)]
        times = [time_ref[i : i + 1, lanes] for i in range(3)]
        for f in range(frames):
            for r in range(rows):
                total = jnp.zeros((SLAB, size), F32)
                for a in range(3):
                    slab = hidden[f + 1, r + a, :, lanes].astype(F32)
                    if a == 1:
                        total = total + slab * (1.0 + times[1])
                    total = total + taps[3 * a + 1] * slab
                    total = total + taps[3 * a] * pltpu.roll(slab, 1, 0)
                    total = total + taps[3 * a + 2] * pltpu.roll(slab, SLAB - 1, 0)
                for a in (0, 2):
                    total = total + times[a] * hidden[f + a, r + 1, :, lanes].astype(F32)
                out_ref[f * rows + r, :, lanes] = total[0:cols].astype(BF16)

    for i in range(4):
        pl.when(sends(i))(halo(i).wait_send)
    for k in range(1, count_r):
        peer = lax.rem(me_r + k, count_r)
        row_copy(peer, me_r).wait_send()
        final_copy(peer, me_r).wait_send()

    def sent(peer, carry):
        prefix_copy(peer, me_t).wait_send()
        return carry

    lax.fori_loop(me_t + 1, count_t, sent, 0)


def front(latent, query_raw, key_raw, value_raw, query_gain, key_gain, space_kernel, time_kernel):
    frames, rows, cols, width = latent.shape
    count_t, count_r = lax.axis_size("tm"), lax.axis_size("row")
    tokens = frames * rows * cols
    part = -(-len(groups_of(width)) // count_r) * LANES
    flat = lambda x: x.reshape(tokens, width)
    dma = pltpu.SemaphoreType.DMA
    vmem = pl.BlockSpec(memory_space=pltpu.VMEM)
    out = pl.pallas_call(
        functools.partial(front_kernel, count_t, count_r, frames, rows, cols),
        out_shape=jax.ShapeDtypeStruct((frames * rows, cols, width), BF16),
        in_specs=[vmem] * 8,
        out_specs=vmem,
        scratch_shapes=[
            pltpu.VMEM((count_r, SLAB, part), STATE_TYPE),
            pltpu.VMEM((count_r, SLAB, part), STATE_TYPE),
            pltpu.VMEM((SLAB, part), STATE_TYPE),
            pltpu.VMEM((count_t, SLAB, part), STATE_TYPE),
            pltpu.VMEM((count_r, SLAB, part), STATE_TYPE),
            pltpu.VMEM((frames + 2, rows + 2, SLAB, width), BF16),
            dma((count_r,)), dma((count_r,)), dma((count_t,)), dma((count_t,)),
            dma((count_r,)), dma((count_r,)), dma((4,)), dma((4,)),
        ],
        compiler_params=pltpu.CompilerParams(
            collective_id=0, has_side_effects=True, vmem_limit_bytes=40 * 1024 * 1024
        ),
    )(
        flat(key_raw), flat(value_raw), flat(query_raw), flat(latent),
        key_gain.reshape(1, width), query_gain.reshape(1, width),
        space_kernel.reshape(9, width), time_kernel,
    )
    return out.reshape(latent.shape)


def per_device(
    latent, query_raw, key_raw, value_raw, query_gain, key_gain, space_kernel, time_kernel,
    first_weight, first_bias, second_weight, second_bias, target_keys, target_values,
):
    frames, rows, cols, width = latent.shape
    blended = front(
        latent, query_raw, key_raw, value_raw, query_gain, key_gain, space_kernel, time_kernel
    )
    gather = functools.partial(lax.all_gather, tiled=True)
    first_full = gather(gather(first_weight, "row", axis=1), "tm", axis=0)
    second_full = gather(gather(second_weight, "row", axis=0), "tm", axis=1)
    keys, values = (gather(x, "row", axis=1) for x in (target_keys, target_values))
    tokens = blended.reshape(-1, width)
    units = jax.nn.silu(dot(tokens, first_full) + first_bias).astype(BF16)
    queries = (dot(units, second_full) + second_bias).astype(BF16)
    split = lambda x: x.reshape(frames, -1, AHEADS, AHEAD_DIM)
    scores = jnp.einsum(
        "cqgd,ckgd->cgqk", split(queries), split(keys), preferred_element_type=F32
    ) * (1.0 / AHEAD_DIM**0.5)
    weights = jnp.exp(scores - jnp.max(scores, axis=-1, keepdims=True))
    row_total = jnp.sum(weights, axis=-1)
    result = jnp.einsum(
        "cgqk,ckgd->cqgd", weights.astype(BF16), split(values), preferred_element_type=F32
    )
    result = result / jnp.transpose(row_total, (0, 2, 1))[..., None]
    attended = result.astype(BF16).reshape(frames, rows, cols, -1)
    return (blended, attended)


def solution(mesh):
    tokens = P("tm", "row", None, None)
    targets = P("tm", "row", None)
    return jax.shard_map(
        per_device,
        mesh=mesh,
        in_specs=(
            tokens, tokens, tokens, tokens, P(), P(), P(), P(),
            P("tm", "row"), P(), P("row", "tm"), P(), targets, targets,
        ),
        out_specs=(tokens, tokens),
        check_vma=False,
    )
```

time: 354 us -> 257 us (0.73)
  Pallas kernels: 0 us -> 76 us
  local copies, waits for them, and re-layouts: 52.6 us -> 8.66 us
  blocking collectives: 56.5 us -> 24.8 us
  other arithmetic: 31.7 us -> 1.1 us
  waiting for transfers between devices: 151 us -> 121 us
  starting transfers between devices: 20.4 us -> 0.19 us
  matrix products: 25.4 us -> 10.6 us
    pallas_call x0 -> x1, Pallas kernels: none -> 76 us  [front(): pl.pallas_call(functools.partial(front_kernel, count_t, count_r, frames,...]
    all_gather x4 -> x5, waiting for transfers between devices: 94 us -> 119 us  [the longest x2 71.5 us: per_device(): first_full = gather(gather(first_weight, 'row', axis=1), 'tm', axis=0)]
    unnamed x7 -> x5, waiting for transfers between devices: 27 us -> 2.09 us
    psum x1 -> x0, blocking collectives: 20.5 us -> none  [per_device(): block_state, block_keys = lax.psum((local_state, local_keys), 'row')]
    reshape x12 -> x5, local copies, waits for them, and re-layouts: 21.6 us -> 2.45 us  [the longest x1 1.4 us: per_device(): attended = result.astype(BF16).reshape(frames, rows, cols, -1)]
    all_to_all x1 -> x0, blocking collectives: 15.8 us -> none  [per_device(): lax.all_to_all(result, 'row', split_axis=1, concat_axis=2, tiled=True)]
    all_to_all x3 -> x0, waiting for transfers between devices: 15.2 us -> none  [the longest x1 15.2 us: per_device(): lax.all_to_all(query_grid, 'row', split_axis=2, concat_axis=1, tiled=True)]
    dot_general x6 -> x3, matrix products: 25.4 us -> 10.6 us  [the longest x1 8.71 us: dot(): return jnp.dot(left, right, preferred_element_type=F32)]
  transfers between devices with their start and end apart: 13 -> 5, of which waited for: 8 -> 4; matrix products, arithmetic and copies ran while one was open for 22% -> 2% of each run, Pallas kernels for 0% -> 30%
where the time goes in v1:
time: 257 us
  waiting for transfers between devices  121 us (47%)
  Pallas kernels  76 us (30%)
  blocking collectives  24.8 us (10%)
  between operations  14 us (5%)
  matrix products  10.6 us (4%)
  local copies, waits for them, and re-layouts  8.66 us (3%)
    pallas_call x1, Pallas kernels, front(): pl.pallas_call(functools.partial(front_kernel, count_t, count_r, frames,...  76 us
    all_gather x2, waiting for transfers between devices, per_device(): first_full = gather(gather(first_weight, 'row', axis=1), 'tm', axis=0)  71.5 us
    all_gather x1, waiting for transfers between devices, per_device(): second_full = gather(gather(second_weight, 'row', axis=0), 'tm', axis=1)  41.8 us
    all_gather x1, blocking collectives, per_device(): second_full = gather(gather(second_weight, 'row', axis=0), 'tm', axis=1)  24.8 us
    dot_general x1, matrix products, dot(): return jnp.dot(left, right, preferred_element_type=F32)  8.71 us
    all_gather x2, waiting for transfers between devices, per_device(): gather(x, 'row', axis=1)  6.01 us
  transfers between devices with their start and end apart: 5, of which 4 were waited for; matrix products, arithmetic and copies ran while one was open for 2% of the time, Pallas kernels for 30%

profile of v1, /device:TPU:0, one launch (start us, length us, event | category | flops | bytes accessed | tf_op | source)
XLA Modules:
  0.0 256.8 jit_solution(8349180054891928761)
XLA Ops:
  7.3 0.7 all-gather.6.cloned.1.call-update
  8.0 0.0 all-gather.12.cloned.1.call-start
  8.0 0.7 all-gather.12.cloned.1.call-update
  8.7 0.0 all-gather.14.cloned.1.call-start
  8.8 0.7 all-gather.14.cloned.1.call-update
  9.5 0.0 all-gather.10.cloned.1.call-start
  9.5 24.8 %all_gather.20 = bf16[2048,160]{0,1:T(8,128)(2,1)} all-gather(bf16[512,160]{0,1:T(8,128)(2,1)} %param.24), channel_id=1, replica_groups=mesh['tm'=8,'row'=4] {'row'}, dimensions={0}, use_global_device_ids=true | all-gather | bytes 819200 | tf_op jit(solution)/shard_map/all_gather | solution.py:289
  34.4 0.0 all-gather.8.cloned.1.call-start
  34.4 12.0 %all-gather.6.cloned.1.call-done = bf16[280,2048]{1,0:T(8,128)(2,1)} async-done(((bf16[280,512]{1,0:T(8,128)(2,1)}), bf16[280,2048]{1,0:T(8,128)(2,1)}) %all-gather.6.cloned.1.call-update) | async-done | bytes 1146896 | tf_op jit(solution)/shard_map/all_gather | solution.py:288
  46.6 1.1 copy-done.3
  47.7 76.0 %shard_map.149 = bf16[4,40,2240]{2,1,0:T(8,128)(2,1)S(1)} custom-call(bf16[160,2240]{1,0:T(8,128)(2,1)S(1)} %bitcast.24, bf16[160,2240]{1,0:T(8,128)(2,1)S(1)} %bitcast.25, bf16[160,2240]{1,0:T(8,128)(2,1)S(1)} %bitcast.26, bf16[160,2240]{1,0:T(8,128)(2,1)S(1)} %bitcast.27, f32[1,2240]{1,0:T(1,128)S(1)} %reshape.48.key_gain, ...), custom_call_target="tpu_custom_call" | custom-call | tf_op jit(solution)/shard_map/pallas_call | solution.py:253
  123.7 1.6 copy.19
  125.3 6.0 %all-gather.14.cloned.1.call-done = bf16[2,256,1280]{2,1,0:T(8,128)(2,1)} async-done(((bf16[2,64,1280]{2,1,0:T(8,128)(2,1)}), bf16[2,256,1280]{2,1,0:T(8,128)(2,1)}) %all-gather.14.cloned.1.call-update) | async-done | bytes 1310736 | tf_op jit(solution)/shard_map/all_gather | solution.py:290
  131.3 2.4 copy.21
  133.8 41.8 %all-gather.10.cloned.1.call-done = bf16[2048,1280]{0,1:T(8,128)(2,1)} async-done(((bf16[2048,160]{0,1:T(8,128)(2,1)}), bf16[2048,1280]{0,1:T(8,128)(2,1)}) %all-gather.10.cloned.1.call-update) | async-done | bytes 5242896 | tf_op jit(solution)/shard_map/all_gather | solution.py:289
  175.5 59.5 %all-gather.8.cloned.1.call-done = bf16[2240,2048]{1,0:T(8,128)(2,1)} async-done(((bf16[280,2048]{1,0:T(8,128)(2,1)}), bf16[2240,2048]{1,0:T(8,128)(2,1)}) %all-gather.8.cloned.1.call-update) | async-done | bytes 9175056 | tf_op jit(solution)/shard_map/all_gather | solution.py:288
  235.0 8.7 %fusion = bf16[160,1280]{1,0:T(8,128)(2,1)S(1)} fusion(bf16[2048,1280]{0,1:T(8,128)(2,1)} %all-gather.10.cloned.1.call-done, bf16[160,2240]{1,0:T(8,128)(2,1)S(1)} %bitcast.22, bf16[2240,2048]{1,0:T(8,128)(2,1)} %all-gather.8.cloned.1.call-done, f32[2048]{0:T(1024)S(1)} %copy-done.9, f32[1280]{0:T(1024)S(1)} %copy-done.10), kind=kOutput, calls=%fused_computation.4 | convolution fusion | flops 2309242880 | bytes 15557632 | tf_op jit(solution)/shard_map/dot_general | solution.py:37
  243.8 1.0 reshape.52
  244.8 0.9 multiply_reduce_fusion
  245.6 1.1 fusion.1
  246.8 1.0 fusion.4
  247.8 0.2 copy.22
  248.0 1.4 reshape.55
  249.4 0.9 copy.28
  (28 shorter events, 0.2 us)
Async XLA Ops:
  7.2 39.3 %copy-start.6 = (f32[3,3,2240]{2,1,0:T(4,128)S(1)}, f32[3,3,2240]{2,1,0:T(4,128)}, u32[]{:S(2)}) copy-start(f32[3,3,2240]{2,1,0:T(4,128)} %param.20) | copy-start | bytes 241924
  7.2 39.3 %copy-start.7 = (f32[2240]{0:T(1024)S(1)}, f32[2240]{0:T(1024)}, u32[]{:S(2)}) copy-start(f32[2240]{0:T(1024)} %param.19) | copy-start | bytes 26884
  7.2 39.3 %copy-start.8 = (f32[2240]{0:T(1024)S(1)}, f32[2240]{0:T(1024)}, u32[]{:S(2)}) copy-start(f32[2240]{0:T(1024)} %param.18) | copy-start | bytes 26884
  7.2 39.4 %copy-start = (bf16[2,2,40,2240]{3,2,1,0:T(8,128)(2,1)S(1)}, bf16[2,2,40,2240]{3,2,1,0:T(8,128)(2,1)}, u32[]{:S(2)}) copy-start(bf16[2,2,40,2240]{3,2,1,0:T(8,128)(2,1)} %param.16) | copy-start | bytes 2150404
  7.2 39.4 %copy-start.1 = (bf16[2,2,40,2240]{3,2,1,0:T(8,128)(2,1)S(1)}, bf16[2,2,40,2240]{3,2,1,0:T(8,128)(2,1)}, u32[]{:S(2)}) copy-start(bf16[2,2,40,2240]{3,2,1,0:T(8,128)(2,1)} %param.17) | copy-start | bytes 2150404
  7.2 39.4 %copy-start.2 = (bf16[2,2,40,2240]{3,2,1,0:T(8,128)(2,1)S(1)}, bf16[2,2,40,2240]{3,2,1,0:T(8,128)(2,1)}, u32[]{:S(2)}) copy-start(bf16[2,2,40,2240]{3,2,1,0:T(8,128)(2,1)} %param.15) | copy-start | bytes 2150404
  7.2 39.4 %copy-start.4 = (f32[3,2240]{1,0:T(4,128)S(1)}, f32[3,2240]{1,0:T(4,128)}, u32[]{:S(2)}) copy-start(f32[3,2240]{1,0:T(4,128)} %time_ref.1) | copy-start | bytes 80644
  7.2 39.2 %all-gather.6.cloned.1.call-start = ((), (), s32[]{:S(2)}) async-start(), calls=%async_computation | async-start | bytes 1433600 | tf_op jit(solution)/shard_map/all_gather | solution.py:288
  8.0 115.8 %all-gather.12.cloned.1.call-start = ((), (), s32[]{:S(2)}) async-start(), calls=%async_computation.3 | async-start | bytes 1638400 | tf_op jit(solution)/shard_map/all_gather | solution.py:290
  8.7 122.6 %all-gather.14.cloned.1.call-start = ((), (), s32[]{:S(2)}) async-start(), calls=%async_computation.4 | async-start | bytes 1638400 | tf_op jit(solution)/shard_map/all_gather | solution.py:290
  9.5 166.1 %all-gather.10.cloned.1.call-start = ((), (), s32[]{:S(2)}) async-start(), calls=%async_computation.2 | async-start | bytes 5898240 | tf_op jit(solution)/shard_map/all_gather | solution.py:289
  34.4 200.7 %all-gather.8.cloned.1.call-start = ((), (), s32[]{:S(2)}) async-start(), calls=%async_computation.1 | async-start | bytes 10321920 | tf_op jit(solution)/shard_map/all_gather | solution.py:288
  46.6 1.1 copy-start.3
  123.7 111.3 %copy-start.9 = (f32[2048]{0:T(1024)S(1)}, f32[2048]{0:T(1024)}, u32[]{:S(2)}) copy-start(f32[2048]{0:T(1024)} %param.23) | copy-start | bytes 24580
  123.7 111.3 %copy-start.10 = (f32[1280]{0:T(1024)S(1)}, f32[1280]{0:T(1024)}, u32[]{:S(2)}) copy-start(f32[1280]{0:T(1024)} %param.25) | copy-start | bytes 15364
  244.7 2.0 copy-start.5
Sparse Core Ops, SparseCore 0:
  9.6 36.7 all-gather.5
  48.0 48.1 all-gather.11
  97.8 33.5 all-gather.13
  133.1 42.4 all-gather.9
  177.3 57.7 all-gather.7

commit v2 on v1

--- a/solution.py
+++ b/solution.py
@@ -13,6 +13,8 @@
 AHEAD_DIM = 80
 LANES = 128
 SLAB = 48
+HELD_BEHIND = 22
+CUBE = 8
 STATE_TYPE = jnp.float32
 F32, BF16 = jnp.float32, jnp.bfloat16
 MESH = pl.DeviceIdType.MESH
@@ -55,10 +57,15 @@
 def front_kernel(
     count_t, count_r, frames, rows, cols,
     key_ref, value_ref, query_ref, latent_ref, key_gain, query_gain, space_ref, time_ref,
-    out_ref,
-    state, row_in, mine, before, final, hidden,
-    rs_send, rs_recv, p_send, p_recv, g_send, g_recv, h_send, h_recv,
+    *others,
 ):
+    held = len(others) - HELD_BEHIND
+    shared, (out_ref, *gathered) = others[: held // 2], others[held // 2 : held + 1]
+    (
+        state, row_in, mine, before, final, hidden,
+        rs_send, rs_recv, p_send, p_recv, g_send, g_recv, h_send, h_recv,
+        own_sem, line_send, side_send, pair_send, full_recv, kv_send, kv_recv,
+    ) = others[held + 1 :]
     me_t, me_r = lax.axis_index("tm"), lax.axis_index("row")
     width = key_ref.shape[1]
     groups = groups_of(width)
@@ -77,6 +84,157 @@
         pl.semaphore_signal(
             barrier, inc=1, device_id={"row": lax.rem(me_r + k, count_r)}, device_id_type=MESH
         )
+
+    kv_in, kv_out = shared[:2], gathered[:2]
+    w_in, w_out = shared[2:], gathered[2:]
+    sent_copies = []
+    own_copies = []
+
+    def w_slot(a, r, t):
+        return w_out[a].at[r, t] if a == 0 else w_out[a].at[t, r]
+
+    def kv_slot(a, r):
+        return kv_out[a].at[:, r]
+
+    def run(condition, action):
+        if condition is None:
+            action()
+        else:
+            pl.when(condition)(action)
+
+    def send(condition, source, target, send_sem, recv_sem, device):
+        def copy():
+            return pltpu.make_async_remote_copy(
+                src_ref=source(), dst_ref=target(), send_sem=send_sem(), recv_sem=recv_sem(),
+                device_id=device, device_id_type=MESH,
+            )
+
+        run(condition, lambda: copy().start())
+        sent_copies.append((condition, lambda: copy().wait_send()))
+
+    def arrive(condition, slot, recv_sem):
+        def wait():
+            pltpu.make_async_remote_copy(
+                src_ref=slot(), dst_ref=slot(), send_sem=own_sem.at[0], recv_sem=recv_sem(),
+                device_id={"row": lax.rem(me_r + 1, count_r)}, device_id_type=MESH,
+            ).wait_recv()
+
+        run(condition, wait)
+
+    def reach(d):
+        if d == 0:
+            return [(None, me_r)]
+        return [(me_r >= d, me_r - d), (me_r < count_r - d, me_r + d)]
+
+    def both(first, second):
+        return second if first is None else jnp.logical_and(first, second)
+
+    def onward(d, a, source, slot, sems, recv):
+        for index, (valid, r) in enumerate(reach(d)):
+            for step in (-1, 1) if d == 0 else ((1,) if index == 0 else (-1,)):
+                inside = (me_r < count_r - 1) if step > 0 else (me_r > 0)
+                lane = (step + 1) // 2
+                send(
+                    both(valid, inside),
+                    lambda a=a, r=r: source(a, r),
+                    lambda a=a, r=r: slot(a, r),
+                    lambda a=a, r=r, lane=lane: sems.at[a, r, lane],
+                    lambda a=a, r=r: recv(a, r),
+                    {"row": me_r + step},
+                )
+
+    flip = lambda bits: lax.bitwise_xor(me_t, jnp.int32(bits))
+
+    def pair(valid, a, r, t, source):
+        send(
+            valid, source, lambda: w_slot(a, r, t), lambda: pair_send.at[a, r, t],
+            lambda: full_recv.at[a, r, t], {"tm": flip(1)},
+        )
+
+    def weights_line(d):
+        def source(a, r):
+            return w_in[a] if d == 0 else w_slot(a, r, me_t)
+
+        for a in range(len(w_in)):
+            if d > 0:
+                for valid, r in reach(d):
+                    arrive(
+                        valid, lambda a=a, r=r: w_slot(a, r, me_t),
+                        lambda a=a, r=r: full_recv.at[a, r, me_t],
+                    )
+            onward(
+                d, a, source, lambda a, r: w_slot(a, r, me_t), line_send,
+                lambda a, r: full_recv.at[a, r, me_t],
+            )
+            for valid, r in reach(d):
+                for side, bits in ((0, 2), (1, 4)):
+                    send(
+                        valid,
+                        lambda a=a, r=r: source(a, r),
+                        lambda a=a, r=r: w_slot(a, r, me_t),
+                        lambda a=a, r=r, side=side: side_send.at[a, r, side, 0],
+                        lambda a=a, r=r: full_recv.at[a, r, me_t],
+                        {"tm": flip(bits)},
+                    )
+                pair(valid, a, r, me_t, lambda a=a, r=r: source(a, r))
+
+    def weights_plane(d):
+        for a in range(len(w_in)):
+            for valid, r in reach(d):
+                for side, bits, other in ((1, 2, 4), (0, 4, 2)):
+                    t = flip(bits)
+                    slot = lambda a=a, r=r, t=t: w_slot(a, r, t)
+                    recv = lambda a=a, r=r, t=t: full_recv.at[a, r, t]
+                    arrive(valid, slot, recv)
+                    send(
+                        both(valid, lax.rem(r, 2) == 1 - side), slot, slot,
+                        lambda a=a, r=r, side=side: side_send.at[a, r, side, 1],
+                        recv, {"tm": flip(other)},
+                    )
+                    pair(valid, a, r, t, slot)
+
+    def weights_corner(d):
+        for a in range(len(w_in)):
+            for valid, r in reach(d):
+                t = flip(6)
+                slot = lambda a=a, r=r, t=t: w_slot(a, r, t)
+                arrive(valid, slot, lambda a=a, r=r, t=t: full_recv.at[a, r, t])
+                pair(valid, a, r, t, slot)
+
+    def weights_rest():
+        for a in range(len(w_in)):
+            for r in range(count_r):
+                for bits in (1, 3, 5, 7):
+                    t = flip(bits)
+                    arrive(
+                        None, lambda a=a, r=r, t=t: w_slot(a, r, t),
+                        lambda a=a, r=r, t=t: full_recv.at[a, r, t],
+                    )
+
+    def targets_line(d):
+        def source(a, r):
+            return kv_in[a] if d == 0 else kv_slot(a, r)
+
+        for a in range(2):
+            if d > 0:
+                for valid, r in reach(d):
+                    arrive(
+                        valid, lambda a=a, r=r: kv_slot(a, r), lambda a=a, r=r: kv_recv.at[a, r]
+                    )
+            onward(d, a, source, kv_slot, kv_send, lambda a, r: kv_recv.at[a, r])
+
+    for a in range(2):
+        own_copies.append((kv_in[a], kv_slot(a, me_r)))
+    for a in range(len(w_in)):
+        own_copies.append((w_in[a], w_slot(a, me_r, me_t)))
+    own_copies = [
+        pltpu.make_async_copy(source, target, own_sem.at[i])
+        for i, (source, target) in enumerate(own_copies)
+    ]
+    for copy in own_copies:
+        copy.start()
+    pl.semaphore_wait(barrier, count_t - 1 + count_r - 1)
+    weights_line(0)
 
     state[...] = jnp.zeros_like(state)
     for index, (start, size) in enumerate(groups):
@@ -97,8 +255,6 @@
             STATE_TYPE
         )
 
-    pl.semaphore_wait(barrier, count_t - 1 + count_r - 1)
-
     def row_copy(peer, slot):
         return pltpu.make_async_remote_copy(
             src_ref=state.at[peer], dst_ref=row_in.at[slot],
@@ -108,6 +264,8 @@
 
     for k in range(1, count_r):
         row_copy(lax.rem(me_r + k, count_r), me_r).start()
+    weights_line(1)
+    targets_line(0)
     total = state[me_r].astype(F32)
     for k in range(1, count_r):
         peer = lax.rem(me_r + k, count_r)
@@ -152,6 +310,7 @@
 
     for k in range(1, count_r):
         final_copy(lax.rem(me_r + k, count_r), me_r).start()
+    weights_plane(0)
     for k in range(1, count_r):
         final_arrival(lax.rem(me_r + k, count_r)).wait_recv()
 
@@ -159,13 +318,13 @@
         mask = same_head(size)
         ones = mask.astype(BF16)
         lanes = pl.ds(start, size)
-        held = final[index // per_part, :, pl.ds((index % per_part) * LANES, size)].astype(F32)
+        table_in = final[index // per_part, :, pl.ds((index % per_part) * LANES, size)].astype(F32)
         feat = features(query_ref[:, lanes], query_gain[:, lanes], ones)
         high, low = parts(feat)
-        table = jnp.concatenate([held[0:HEAD_DIM]] * (size // HEAD_DIM), axis=0) * mask
+        table = jnp.concatenate([table_in[0:HEAD_DIM]] * (size // HEAD_DIM), axis=0) * mask
         table_high, table_low = parts(table)
         numerator = dot(high, table_high) + dot(low, table_high) + dot(high, table_low)
-        denominator = head_sums(feat * held[HEAD_DIM : HEAD_DIM + 1], ones) + 1e-06
+        denominator = head_sums(feat * table_in[HEAD_DIM : HEAD_DIM + 1], ones) + 1e-06
         mixed = latent_ref[:, lanes].astype(F32) + numerator / denominator
         for f in range(frames):
             for r in range(rows):
@@ -175,6 +334,10 @@
                 )
                 hidden[f + 1, r + 1, :, lanes] = padded.astype(BF16)
 
+    for d in range(2, count_r):
+        if d == 2:
+            weights_line(d)
+    weights_corner(0)
     body_f, body_r = pl.ds(1, frames), pl.ds(1, rows)
     moves = (
         ("tm", me_t, count_t, -1, hidden.at[1, body_r], hidden.at[frames + 1, body_r]),
@@ -210,6 +373,7 @@
     for i in range(4):
         pl.when(receives(i))(halo(i).wait_recv)
 
+    weights_plane(1)
     for start, size in groups:
         lanes = pl.ds(start, size)
         taps = [space_ref[i : i + 1, lanes] for i in range(9)]
@@ -228,6 +392,19 @@
                     total = total + times[a] * hidden[f + a, r + 1, :, lanes].astype(F32)
                 out_ref[f * rows + r, :, lanes] = total[0:cols].astype(BF16)
 
+    for d in range(3, count_r):
+        weights_line(d)
+    targets_line(1)
+    weights_corner(1)
+    for d in range(2, count_r):
+        weights_plane(d)
+        targets_line(d)
+        weights_corner(d)
+    weights_rest()
+    for copy in own_copies:
+        copy.wait()
+    for condition, action in sent_copies:
+        run(condition, action)
     for i in range(4):
         pl.when(sends(i))(halo(i).wait_send)
     for k in range(1, count_r):
@@ -242,7 +419,10 @@
     lax.fori_loop(me_t + 1, count_t, sent, 0)
 
 
-def front(latent, query_raw, key_raw, value_raw, query_gain, key_gain, space_kernel, time_kernel):
+def front(
+    latent, query_raw, key_raw, value_raw, query_gain, key_gain, space_kernel, time_kernel,
+    targets, weights,
+):
     frames, rows, cols, width = latent.shape
     count_t, count_r = lax.axis_size("tm"), lax.axis_size("row")
     tokens = frames * rows * cols
@@ -250,11 +430,17 @@
     flat = lambda x: x.reshape(tokens, width)
     dma = pltpu.SemaphoreType.DMA
     vmem = pl.BlockSpec(memory_space=pltpu.VMEM)
-    out = pl.pallas_call(
+    anywhere = pl.BlockSpec(memory_space=pl.ANY)
+    shared = tuple(targets) + tuple(weights)
+    kept = [(x.shape[0], count_r) + x.shape[1:] for x in targets]
+    for x, lead in zip(weights, ((count_r, count_t), (count_t, count_r))):
+        kept.append(lead + x.shape)
+    shapes = [(frames * rows, cols, width)] + kept
+    out, *full = pl.pallas_call(
         functools.partial(front_kernel, count_t, count_r, frames, rows, cols),
-        out_shape=jax.ShapeDtypeStruct((frames * rows, cols, width), BF16),
-        in_specs=[vmem] * 8,
-        out_specs=vmem,
+        out_shape=[jax.ShapeDtypeStruct(shape, BF16) for shape in shapes],
+        in_specs=[vmem] * 8 + [anywhere] * len(shared),
+        out_specs=[vmem] + [anywhere] * len(shared),
         scratch_shapes=[
             pltpu.VMEM((count_r, SLAB, part), STATE_TYPE),
             pltpu.VMEM((count_r, SLAB, part), STATE_TYPE),
@@ -264,6 +450,9 @@
             pltpu.VMEM((frames + 2, rows + 2, SLAB, width), BF16),
             dma((count_r,)), dma((count_r,)), dma((count_t,)), dma((count_t,)),
             dma((count_r,)), dma((count_r,)), dma((4,)), dma((4,)),
+            dma((4,)), dma((2, count_r, 2)), dma((2, count_r, 2, 2)),
+            dma((2, count_r, count_t)), dma((2, count_r, count_t)),
+            dma((2, count_r, 2)), dma((2, count_r)),
         ],
         compiler_params=pltpu.CompilerParams(
             collective_id=0, has_side_effects=True, vmem_limit_bytes=40 * 1024 * 1024
@@ -271,9 +460,9 @@
     )(
         flat(key_raw), flat(value_raw), flat(query_raw), flat(latent),
         key_gain.reshape(1, width), query_gain.reshape(1, width),
-        space_kernel.reshape(9, width), time_kernel,
+        space_kernel.reshape(9, width), time_kernel, *shared,
     )
-    return out.reshape(latent.shape)
+    return out.reshape(latent.shape), full
 
 
 def per_device(
@@ -281,16 +470,29 @@
     first_weight, first_bias, second_weight, second_bias, target_keys, target_values,
 ):
     frames, rows, cols, width = latent.shape
-    blended = front(
-        latent, query_raw, key_raw, value_raw, query_gain, key_gain, space_kernel, time_kernel
+    count_t = lax.axis_size("tm")
+    gather = functools.partial(lax.all_gather, tiled=True)
+    weights = (first_weight, second_weight) if count_t == CUBE else ()
+    blended, (keys, values, *full) = front(
+        latent, query_raw, key_raw, value_raw, query_gain, key_gain, space_kernel, time_kernel,
+        (target_keys, target_values), weights,
     )
-    gather = functools.partial(lax.all_gather, tiled=True)
-    first_full = gather(gather(first_weight, "row", axis=1), "tm", axis=0)
-    second_full = gather(gather(second_weight, "row", axis=0), "tm", axis=1)
-    keys, values = (gather(x, "row", axis=1) for x in (target_keys, target_values))
+    if full:
+        first_full = full[0].reshape(full[0].shape[0], width, -1)
+        second_full = full[1].reshape(full[1].shape[0], -1, full[1].shape[-1])
+    else:
+        first_full = gather(first_weight, "tm", axis=0)
+        first_full = gather(first_full, "row", axis=1)[None]
+        second_full = gather(second_weight, "row", axis=0)
+        second_full = gather(second_full, "tm", axis=1)[None]
     tokens = blended.reshape(-1, width)
-    units = jax.nn.silu(dot(tokens, first_full) + first_bias).astype(BF16)
-    queries = (dot(units, second_full) + second_bias).astype(BF16)
+
+    def layer(left, right, bias):
+        product = jnp.einsum("mk,rkn->mrn", left, right, preferred_element_type=F32)
+        return product.reshape(left.shape[0], -1) + bias
+
+    units = jax.nn.silu(layer(tokens, first_full, first_bias)).astype(BF16)
+    queries = layer(units, second_full, second_bias).astype(BF16)
     split = lambda x: x.reshape(frames, -1, AHEADS, AHEAD_DIM)
     scores = jnp.einsum(
         "cqgd,ckgd->cgqk", split(queries), split(keys), preferred_element_type=F32

time: 257 us -> 203 us (0.79)
  waiting for transfers between devices: 121 us -> 0 us
  Pallas kernels: 76 us -> 133 us
  local copies, waits for them, and re-layouts: 8.66 us -> 47.4 us
  blocking collectives: 24.8 us -> 0 us
  between operations: 14 us -> 0.73 us
  matrix products: 10.6 us -> 17.2 us
    all_gather x5 -> x0, waiting for transfers between devices: 119 us -> none  [the longest x2 71.5 us: per_device(): first_full = gather(gather(first_weight, 'row', axis=1), 'tm', axis=0)]
    pallas_call x1, Pallas kernels: 76 us -> 133 us  [front(): pl.pallas_call(functools.partial(front_kernel, count_t, count_r, frames,...]
    all_gather x1 -> x0, blocking collectives: 24.8 us -> none  [per_device(): second_full = gather(gather(second_weight, 'row', axis=0), 'tm', axis=1)]
    reshape x0 -> x2, local copies, waits for them, and re-layouts: none -> 23 us  [the longest x1 12.2 us: per_device(): first_full = full[0].reshape(full[0].shape[0], width, -1)]
    unnamed x23 -> x28, local copies, waits for them, and re-layouts: 2.02 us -> 10.9 us
    reshape x1 -> x3, local copies, waits for them, and re-layouts: 0.99 us -> 9.25 us  [per_device(): split = lambda x: x.reshape(frames, -1, AHEADS, AHEAD_DIM)]
    all_gather x2 -> x0, local copies, waits for them, and re-layouts: 4.02 us -> none  [per_device(): gather(x, 'row', axis=1)]
    dot_general x1, matrix products: 0.87 us -> 3.99 us  [per_device(): jnp.einsum('cqgd,ckgd->cgqk', split(queries), split(keys), preferred_elem...]
  transfers between devices with their start and end apart: 5 -> 0, of which waited for: 4 -> 0; matrix products, arithmetic and copies ran while one was open for 2% -> 0% of each run, Pallas kernels for 30% -> 0%
where the time goes in v2:
time: 203 us; the launch traced here: 201 us
  Pallas kernels  133 us (66%)
  local copies, waits for them, and re-layouts  47.4 us (23%)
  matrix products  17.2 us (8%)
  other arithmetic  2.87 us (1%)
    pallas_call x1, Pallas kernels, front(): pl.pallas_call(functools.partial(front_kernel, count_t, count_r, frames,...  133 us
    reshape x1, local copies, waits for them, and re-layouts, per_device(): first_full = full[0].reshape(full[0].shape[0], width, -1)  12.2 us
    unnamed x28, local copies, waits for them, and re-layouts  10.9 us
    reshape x1, local copies, waits for them, and re-layouts, per_device(): second_full = full[1].reshape(full[1].shape[0], -1, full[1].shape[-1])  10.8 us
    dot_general x1, matrix products, layer(): product = jnp.einsum('mk,rkn->mrn', left, right, preferred_element_type=F32)  10.3 us
    reshape x3, local copies, waits for them, and re-layouts, per_device(): split = lambda x: x.reshape(frames, -1, AHEADS, AHEAD_DIM)  9.25 us

profile of v2, /device:TPU:0, one launch (start us, length us, event | category | flops | bytes accessed | tf_op | source)
XLA Modules:
  0.0 201.1 jit_solution(1403448706431903776)
XLA Ops:
  0.6 0.7 reshape.58.key_gain
  2.1 0.9 reshape.60.space_ref
  3.0 1.0 copy.21.others_3_
  4.1 1.1 copy-done
  5.2 1.1 copy-done.1
  6.3 1.1 copy-done.2
  7.4 1.1 copy-done.3
  8.5 1.0 copy-done.6
  9.5 1.0 copy-done.7
  10.5 1.0 copy-done.8
  11.4 0.8 copy-done.9
  12.2 132.8 %shard_map.149 = (bf16[4,40,2240]{2,1,0:T(8,128)(2,1)S(1)}, bf16[2,4,64,1280]{3,2,1,0:T(8,128)(2,1)S(1)}, bf16[2,4,64,1280]{3,2,1,0:T(8,128)(2,1)S(1)}, bf16[4,8...) custom-call(bf16[160,2240]{1,0:T(8,128)(2,1)S(1)} %bitcast.28, bf16[160,2240]{1,0:T(8,128)(2,1)S(1)} %bitcast.29, ...), custom_call_target="tpu_custom_call" | custom-call | tf_op jit(solution)/shard_map/pallas_call | solution.py:439
  145.0 0.9 copy-done.4
  145.9 4.2 %reshape.66 = bf16[2,256,16,80]{3,2,1,0:T(8,128)(2,1)} reshape(bf16[2,4,64,1280]{3,2,1,0:T(8,128)(2,1)S(1)} %get-tuple-element.11) | data formatting | bytes 2621440 | tf_op jit(solution)/shard_map/reshape | solution.py:496
  150.0 10.8 %copy.23 = bf16[8,2048,160]{1,2,0:T(8,128)(2,1)} copy(bf16[8,2048,160]{2,1,0:T(8,128)(2,1)} %bitcast.36) | data formatting | bytes 10485760 | tf_op jit(solution)/shard_map/reshape | solution.py:482
  160.8 12.2 %copy.22 = bf16[4,2240,512]{1,2,0:T(8,128)(2,1)} copy(bf16[4,2240,512]{2,1,0:T(8,128)(2,1)} %bitcast.35) | data formatting | bytes 18350080 | tf_op jit(solution)/shard_map/reshape | solution.py:481
  173.0 10.3 %fusion = bf16[160,1280]{1,0:T(8,128)(2,1)S(1)} fusion(bf16[1280,2048]{1,0:T(8,128)(2,1)} %bitcast.37, bf16[160,2240]{1,0:T(8,128)(2,1)S(1)} %bitcast.32, bf16[2048,2240]{1,0:T(8,128)(2,1)} %bitcast.34, f32[2048]{0:T(1024)S(1)} %copy-done.11, f32[1280]{0:T(1024)S(1)} %copy-done.12), kind=kOutput, calls=%fused_computation.4 | convolution fusion | flops 2309242880 | bytes 15557632 | tf_op jit(solution)/shard_map/mk,rkn->mrn/dot_general | solution.py:491
  183.3 1.0 reshape.65
  184.3 4.0 %multiply_reduce_fusion = (f32[2,16,80]{2,1,0:T(8,128)S(1)}, f32[2,16,80,256]{3,2,1,0:T(8,128)}) fusion(bf16[2,256,16,80]{3,2,1,0:T(8,128)(2,1)} %reshape.66, bf16[2,80,16,80]{3,2,1,0:T(8,128)(2,1)S(1)} %reshape.65), kind=kOutput, calls=%fused_computation.2 | convolution fusion | flops 106165760 | bytes 4352000 | tf_op jit(solution)/shard_map/cqgd,ckgd->cgqk/dot_general | solution.py:497
  188.3 4.1 %reshape.62 = bf16[2,256,16,80]{3,2,1,0:T(8,128)(2,1)} reshape(bf16[2,4,64,1280]{3,2,1,0:T(8,128)(2,1)S(1)} %get-tuple-element.8) | data formatting | bytes 2621440 | tf_op jit(solution)/shard_map/reshape | solution.py:496
  192.4 2.9 %fusion.1 = f32[2,16,80]{2,1,0:T(8,128)S(1)} fusion(f32[2,16,80,256]{3,2,1,0:T(8,128)} %get-tuple-element.15, f32[2,16,80]{2,1,0:T(8,128)S(1)} %get-tuple-element.14), kind=kLoop, calls=%fused_computation.5 | loop fusion | flops 1963520 | bytes 2641920 | tf_op jit(solution)/shard_map/reduce_sum | solution.py:501
  195.3 2.9 %divide_convert_fusion = bf16[2,80,16,80]{1,3,2,0:T(8,128)(2,1)S(1)} fusion(f32[2,16,80,256]{3,2,1,0:T(8,128)S(1)} %copy-done.10, f32[2,16,80]{2,1,0:T(8,128)S(1)} %get-tuple-element.14, bf16[2,256,16,80]{3,2,1,0:T(8,128)(2,1)} %reshape.62, f32[2,80,16]{1,2,0:T(8,128)S(1)} %bitcast.38), kind=kOutput, calls=%fused_computation.12 | convolution fusion | flops 107233280 | bytes 4362240 | tf_op jit(solution)/shard_map/cgqk,ckgd->cqgd/dot_general | solution.py:502
  198.8 1.4 reshape.67
  200.2 0.9 copy.43
  (19 shorter events, 1.3 us)
Async XLA Ops:
  4.1 1.1 copy-start
  5.2 1.1 copy-start.1
  6.3 1.1 copy-start.2
  7.4 1.1 copy-start.3
  8.5 1.0 copy-start.6
  9.5 1.0 copy-start.7
  10.5 1.0 copy-start.8
  11.4 0.8 copy-start.9
  145.0 0.9 copy-start.4
  160.8 12.2 %copy-start.5 = (bf16[4,40,2240]{2,1,0:T(8,128)(2,1)S(1)}, bf16[4,40,2240]{2,1,0:T(8,128)(2,1)}, u32[]{:S(2)}) copy-start(bf16[4,40,2240]{2,1,0:T(8,128)(2,1)} %copy-done.4) | copy-start | bytes 2150404
  160.8 12.2 %copy-start.11 = (f32[2048]{0:T(1024)S(1)}, f32[2048]{0:T(1024)}, u32[]{:S(2)}) copy-start(f32[2048]{0:T(1024)} %param.23) | copy-start | bytes 24580
  160.8 12.2 %copy-start.12 = (f32[1280]{0:T(1024)S(1)}, f32[1280]{0:T(1024)}, u32[]{:S(2)}) copy-start(f32[1280]{0:T(1024)} %param.25) | copy-start | bytes 15364
  192.4 2.9 %copy-start.10 = (f32[2,16,80,256]{3,2,1,0:T(8,128)S(1)}, f32[2,16,80,256]{3,2,1,0:T(8,128)}, u32[]{:S(2)}) copy-start(f32[2,16,80,256]{3,2,1,0:T(8,128)} %get-tuple-element.15) | copy-start | bytes 7864324

commit v3 on v2

--- a/solution.py
+++ b/solution.py
@@ -13,7 +13,7 @@
 AHEAD_DIM = 80
 LANES = 128
 SLAB = 48
-HELD_BEHIND = 22
+HELD_BEHIND = 27
 CUBE = 8
 STATE_TYPE = jnp.float32
 F32, BF16 = jnp.float32, jnp.bfloat16
@@ -56,7 +56,7 @@
 
 def front_kernel(
     count_t, count_r, frames, rows, cols,
-    key_ref, value_ref, query_ref, latent_ref, key_gain, query_gain, space_ref, time_ref,
+    key_hbm, value_hbm, query_hbm, latent_hbm, key_gain, query_gain, space_ref, time_ref,
     *others,
 ):
     held = len(others) - HELD_BEHIND
@@ -65,9 +65,21 @@
         state, row_in, mine, before, final, hidden,
         rs_send, rs_recv, p_send, p_recv, g_send, g_recv, h_send, h_recv,
         own_sem, line_send, side_send, pair_send, full_recv, kv_send, kv_recv,
+        key_ref, value_ref, query_ref, latent_ref, load_sem,
     ) = others[held + 1 :]
     me_t, me_r = lax.axis_index("tm"), lax.axis_index("row")
-    width = key_ref.shape[1]
+    width = key_hbm.shape[1]
+    loads = [
+        pltpu.make_async_copy(source, target, load_sem.at[i])
+        for i, (source, target) in enumerate(
+            (
+                (key_hbm, key_ref), (value_hbm, value_ref),
+                (query_hbm, query_ref), (latent_hbm, latent_ref),
+            )
+        )
+    ]
+    for load in loads:
+        load.start()
     groups = groups_of(width)
     per_part = -(-len(groups) // count_r)
 
@@ -235,6 +247,8 @@
         copy.start()
     pl.semaphore_wait(barrier, count_t - 1 + count_r - 1)
     weights_line(0)
+    loads[0].wait()
+    loads[1].wait()
 
     state[...] = jnp.zeros_like(state)
     for index, (start, size) in enumerate(groups):
@@ -314,6 +328,8 @@
     for k in range(1, count_r):
         final_arrival(lax.rem(me_r + k, count_r)).wait_recv()
 
+    loads[2].wait()
+    loads[3].wait()
     for index, (start, size) in enumerate(groups):
         mask = same_head(size)
         ones = mask.astype(BF16)
@@ -374,6 +390,7 @@
         pl.when(receives(i))(halo(i).wait_recv)
 
     weights_plane(1)
+    targets_line(1)
     for start, size in groups:
         lanes = pl.ds(start, size)
         taps = [space_ref[i : i + 1, lanes] for i in range(9)]
@@ -394,11 +411,12 @@
 
     for d in range(3, count_r):
         weights_line(d)
-    targets_line(1)
+    for d in range(2, count_r):
+        targets_line(d)
     weights_corner(1)
     for d in range(2, count_r):
         weights_plane(d)
-        targets_line(d)
+    for d in range(2, count_r):
         weights_corner(d)
     weights_rest()
     for copy in own_copies:
@@ -430,6 +448,7 @@
     flat = lambda x: x.reshape(tokens, width)
     dma = pltpu.SemaphoreType.DMA
     vmem = pl.BlockSpec(memory_space=pltpu.VMEM)
+    outer = pl.BlockSpec(memory_space=pltpu.HBM)
     anywhere = pl.BlockSpec(memory_space=pl.ANY)
     shared = tuple(targets) + tuple(weights)
     kept = [(x.shape[0], count_r) + x.shape[1:] for x in targets]
@@ -439,7 +458,7 @@
     out, *full = pl.pallas_call(
         functools.partial(front_kernel, count_t, count_r, frames, rows, cols),
         out_shape=[jax.ShapeDtypeStruct(shape, BF16) for shape in shapes],
-        in_specs=[vmem] * 8 + [anywhere] * len(shared),
+        in_specs=[outer] * 4 + [vmem] * 4 + [outer] * len(shared),
         out_specs=[vmem] + [anywhere] * len(shared),
         scratch_shapes=[
             pltpu.VMEM((count_r, SLAB, part), STATE_TYPE),
@@ -453,6 +472,7 @@
             dma((4,)), dma((2, count_r, 2)), dma((2, count_r, 2, 2)),
             dma((2, count_r, count_t)), dma((2, count_r, count_t)),
             dma((2, count_r, 2)), dma((2, count_r)),
+            *[pltpu.VMEM((tokens, width), BF16)] * 4, dma((4,)),
         ],
         compiler_params=pltpu.CompilerParams(
             collective_id=0, has_side_effects=True, vmem_limit_bytes=40 * 1024 * 1024
@@ -488,8 +508,8 @@
     tokens = blended.reshape(-1, width)
 
     def layer(left, right, bias):
-        product = jnp.einsum("mk,rkn->mrn", left, right, preferred_element_type=F32)
-        return product.reshape(left.shape[0], -1) + bias
+        pieces = [dot(left, right[i]) for i in range(right.shape[0])]
+        return jnp.concatenate(pieces, axis=1) + bias
 
     units = jax.nn.silu(layer(tokens, first_full, first_bias)).astype(BF16)
     queries = layer(units, second_full, second_bias).astype(BF16)

time: 203 us -> 195 us (0.961)
  local copies, waits for them, and re-layouts: 47.4 us -> 37.1 us
  Pallas kernels: 133 us -> 139 us
    reshape x2 -> x0, local copies, waits for them, and re-layouts: 23 us -> none  [the longest x1 12.2 us: per_device(): first_full = full[0].reshape(full[0].shape[0], width, -1)]
    pallas_call x1, Pallas kernels: 133 us -> 139 us  [front(): pl.pallas_call(functools.partial(front_kernel, count_t, count_r, frames,...]
    concatenate x0 -> x2, local copies, waits for them, and re-layouts: none -> 5.3 us  [layer(): return jnp.concatenate(pieces, axis=1) + bias]
    slice x0 -> x2, local copies, waits for them, and re-layouts: none -> 4.93 us  [layer(): pieces = [dot(left, right[i]) for i in range(right.shape[0])]]
    unnamed x28 -> x30, local copies, waits for them, and re-layouts: 10.9 us -> 14.3 us
    reshape x3 -> x2, local copies, waits for them, and re-layouts: 9.25 us -> 8.22 us  [per_device(): split = lambda x: x.reshape(frames, -1, AHEADS, AHEAD_DIM)]
    dot_general x1 -> x12, matrix products: 10.3 us -> 9.59 us  [dot(): return jnp.dot(left, right, preferred_element_type=F32)]
where the time goes in v3:
time: 195 us
  Pallas kernels  139 us (71%)
  local copies, waits for them, and re-layouts  37.1 us (19%)
  matrix products  16.4 us (8%)
    pallas_call x1, Pallas kernels, front(): pl.pallas_call(functools.partial(front_kernel, count_t, count_r, frames,...  139 us
    unnamed x30, local copies, waits for them, and re-layouts  14.3 us
    dot_general x12, matrix products, dot(): return jnp.dot(left, right, preferred_element_type=F32)  9.59 us
    reshape x2, local copies, waits for them, and re-layouts, per_device(): split = lambda x: x.reshape(frames, -1, AHEADS, AHEAD_DIM)  8.22 us
    concatenate x2, local copies, waits for them, and re-layouts, layer(): return jnp.concatenate(pieces, axis=1) + bias  5.3 us
    slice x2, local copies, waits for them, and re-layouts, layer(): pieces = [dot(left, right[i]) for i in range(right.shape[0])]  4.93 us

profile of v3, /device:TPU:0, one launch (start us, length us, event | category | flops | bytes accessed | tf_op | source)
XLA Modules:
  0.0 194.6 jit_solution(7940351249119534948)
XLA Ops:
  0.6 1.8 copy.21.others_3_
  5.7 1.1 copy-done.1
  6.8 1.1 copy-done.2
  7.9 1.1 copy-done.3
  9.1 1.1 copy-done.4
  10.2 1.0 copy-done.5
  13.8 138.8 %shard_map.149 = (bf16[4,40,2240]{2,1,0:T(8,128)(2,1)S(1)}, bf16[2,4,64,1280]{3,2,1,0:T(8,128)(2,1)S(1)}, bf16[2,4,64,1280]{3,2,1,0:T(8,128)(2,1)S(1)}, bf16[4,8...) custom-call(bf16[160,2240]{1,0:T(8,128)(2,1)S(1)} %bitcast.58, bf16[160,2240]{1,0:T(8,128)(2,1)S(1)} %bitcast.59, ...), custom_call_target="tpu_custom_call" | custom-call | tf_op jit(solution)/shard_map/pallas_call | solution.py:458
  152.6 4.1 %fusion.20 = (bf16[1,8,280,512]{3,2,1,0:T(8,128)(2,1)S(1)}, bf16[1,8,280,512]{3,2,1,0:T(8,128)(2,1)S(1)}, bf16[1,8,280,512]{3,2,1,0:T(8,128)(2,1)S(1)}, bf16[1,8,280,512]{3,2,1,0:T(8,128)(2,1)S(1)}) fusion(bf16[4,8,280,512]{3,2,1,0:T(8,128)(2,1)} %get-tuple-element.9), kind=kLoop, calls=%fused_computation.18 | loop fusion | bytes 18350080 | tf_op jit(solution)/shard_map/slice | solution.py:511
  161.7 1.0 fusion.32
  162.7 1.0 fusion.31
  163.7 1.0 fusion.30
  164.7 1.0 fusion.29
  165.7 1.0 fusion.28
  166.7 1.0 fusion.27
  167.7 1.0 fusion.26
  168.7 2.3 %concatenate.9 = f32[160,1280]{1,0:T(8,128)} concatenate(f32[160,160]{1,0:T(8,128)} %fusion.26, f32[160,160]{1,0:T(8,128)} %fusion.27, f32[160,160]{1,0:T(8,128)} %fusion.28, f32[160,160]{1,0:T(8,128)} %fusion.29, f32[160,160]{1,0:T(8,128)} %fusion.30, f32[160,160]{1,0:T(8,128)} %fusion.31, f32[160,160]{1,0:T(8,128)} %fusion.32, f32[160,160]{1,0:T(8,128)S(1)} %fusion.33), dimensions={1} | concatenate | bytes 1638400 | tf_op jit(solution)/shard_map/concatenate | solution.py:512
  171.0 3.0 %concatenate.10 = f32[2,80,16,80]{3,2,1,0:T(8,128)} reshape(f32[160,1280]{1,0:T(8,128)} %concatenate.9) | data formatting | bytes 1638400 | tf_op jit(solution)/shard_map/concatenate | solution.py:512
  174.0 4.1 %reshape.83 = bf16[2,256,16,80]{3,2,1,0:T(8,128)(2,1)} reshape(bf16[2,4,64,1280]{3,2,1,0:T(8,128)(2,1)S(1)} %get-tuple-element.11) | data formatting | bytes 2621440 | tf_op jit(solution)/shard_map/reshape | solution.py:516
  178.2 3.1 %multiply_reduce_fusion = (f32[2,16,80]{2,1,0:T(8,128)S(1)}, f32[2,16,80,256]{3,2,1,0:T(8,128)S(1)}) fusion(bf16[2,256,16,80]{3,2,1,0:T(8,128)(2,1)} %reshape.83, f32[2,80,16,80]{3,2,1,0:T(8,128)} %concatenate.10, f32[16,80]{1,0:T(8,128)S(1)} %add.26), kind=kOutput, calls=%fused_computation.1 | convolution fusion | flops 106575360 | bytes 4766720 | tf_op jit(solution)/shard_map/cqgd,ckgd->cgqk/dot_general | solution.py:517
  181.4 1.5 copy-done.9
  182.8 1.1 fusion
  183.9 4.1 %reshape.82 = bf16[2,256,16,80]{3,2,1,0:T(8,128)(2,1)} reshape(bf16[2,4,64,1280]{3,2,1,0:T(8,128)(2,1)S(1)} %get-tuple-element.8) | data formatting | bytes 2621440 | tf_op jit(solution)/shard_map/reshape | solution.py:516
  188.1 3.7 %divide_convert_fusion = bf16[2,80,16,80]{1,3,2,0:T(8,128)(2,1)S(1)} fusion(f32[2,16,80,256]{3,2,1,0:T(8,128)} %copy-done.9, f32[2,16,80]{2,1,0:T(8,128)S(1)} %get-tuple-element.26, bf16[2,256,16,80]{3,2,1,0:T(8,128)(2,1)} %reshape.82, f32[2,80,16]{1,2,0:T(8,128)S(1)} %bitcast.76), kind=kOutput, calls=%fused_computation.12 | convolution fusion | flops 107233280 | bytes 4362240 | tf_op jit(solution)/shard_map/cgqk,ckgd->cqgd/dot_general | solution.py:522
  192.3 1.4 reshape.84
  (36 shorter events, 12.3 us)
Async XLA Ops:
  4.8 0.9 copy-start
  5.7 1.1 copy-start.1
  6.8 1.1 copy-start.2
  7.9 1.1 copy-start.3
  9.1 1.1 copy-start.4
  10.2 1.0 copy-start.5
  11.1 1.0 copy-start.6
  12.1 1.0 copy-start.7
  13.1 0.8 copy-start.8
  156.8 3.2 %slice-start = ((s8[8388608]{0:T(1024)(128)(4,1)}), s8[4194304]{0:T(1024)(128)(4,1)S(1)}, s32[]{:S(2)}) async-start(s8[8388608]{0:T(1024)(128)(4,1)} %bitcast.66), calls=%async_computation | async-start | bytes 8388608
  157.9 2.6 %slice-start.1 = ((s8[8388608]{0:T(1024)(128)(4,1)}), s8[4194304]{0:T(1024)(128)(4,1)S(1)}, s32[]{:S(2)}) async-start(s8[8388608]{0:T(1024)(128)(4,1)} %bitcast.66), calls=%async_computation.1 | async-start | bytes 8388608
  158.4 1.1 copy-start.10
  171.0 7.1 %copy-start.11 = (f32[1280]{0:T(1024)S(1)}, f32[1280]{0:T(1024)}, u32[]{:S(2)}) copy-start(f32[1280]{0:T(1024)} %param.25) | copy-start | bytes 15364
  181.3 1.5 copy-start.9
